TPU v7x, 128 devices: a whole 4x4x4 slice. The times are simulated.
128 devices in a mesh: sample: 16 (over x, z_lo, core), ctx: 8 (over y, z_hi).
Axes of the slice: x: 4, y: 4, z: 4 (z_hi: 2, z_lo: 2; z = z_hi * 2 + z_lo), core: 2. Of those that a mesh axis runs over, the one named last changes fastest.
Arguments:
- prompt_query: bfloat16 [4096, 1024], P(('sample', 'ctx')), may hold values from -13 to 13
- prompt_key: bfloat16 [4096, 128], P('ctx'), may hold values from -13 to 13
- prompt_value: bfloat16 [4096, 128], P('ctx'), may hold values from -6 to 6
- prompt_cotangent: bfloat16 [4096, 1024], P(('sample', 'ctx')), may hold values from -96 to 96
- prompt_output: bfloat16 [4096, 1024], P(('sample', 'ctx')), may hold values from -1.5 to 1.5
- response_query: bfloat16 [16, 2048, 1024], P('sample', 'ctx'), may hold values from -13 to 13
- response_key: bfloat16 [16, 2048, 128], P('sample', 'ctx'), may hold values from -6 to 6
- response_value: bfloat16 [16, 2048, 128], P('sample', 'ctx'), may hold values from -6 to 6
- response_cotangent: bfloat16 [16, 2048, 1024], P('sample', 'ctx'), may hold values from -96 to 96
- response_output: bfloat16 [16, 2048, 1024], P('sample', 'ctx'), may hold values from -1.5 to 1.5
- lengths: int32 [16], P('sample'), may hold values from 1 to 2048, 16384 in all
Outputs:
- prompt_query_grad: bfloat16 [4096, 1024], P(('sample', 'ctx'))
- prompt_key_grad: bfloat16 [4096, 128], P(('sample', 'ctx'))
- prompt_value_grad: bfloat16 [4096, 128], P(('sample', 'ctx'))
- response_query_grad: bfloat16 [16, 2048, 1024], P('sample', 'ctx')
- response_key_grad: bfloat16 [16, 2048, 128], P('sample', 'ctx')
- response_value_grad: bfloat16 [16, 2048, 128], P('sample', 'ctx')
Inputs may be any that keep to these rules, and one draw needn't show every extreme that they name: The 16 lengths sum to 16384 and one of them equals 2048.
All inputs are finite; a program needn't handle non-finite values. No bound on the sum of `lengths` on one device may be relied on, other than what follows from the above.
Results may differ from a plain program's by a relative error of at most 0.015.
Values may be sent and summed in bfloat16 or wider, within the bound.
A program may use at most 64 MiB of HBM per device.

v0:
```python
import jax
import jax.numpy as jnp
from jax import lax
from jax.sharding import PartitionSpec as P

masked_value = -1e30


def scores_of(queries, key_rows):
    scaling = key_rows.shape[1] ** (-0.5)
    return (
        jnp.einsum("nhd,md->hnm", queries, key_rows, preferred_element_type=jnp.float32) * scaling
    )


def attend_back(
    queries,
    grad_out,
    outputs,
    key_rows,
    values,
    num_blocks,
    block_size,
    allowed_fn,
    live_rows,
    key_grads,
    value_grads,
):
    head_count = queries.shape[1]
    row_count = queries.shape[0]
    scaling = key_rows.shape[1] ** (-0.5)

    def stats_step(step_id, state_now):
        row_max, row_sum = state_now
        offset = step_id * block_size
        mask = allowed_fn(offset)[None]
        key_block = lax.dynamic_slice_in_dim(key_rows, offset, block_size, 0)
        scores = jnp.where(mask, scores_of(queries, key_block), masked_value)
        new_max = jnp.maximum(row_max, jnp.max(scores, axis=2))
        weights = jnp.where(mask, jnp.exp(scores - new_max[:, :, None]), 0.0)
        return (new_max, row_sum * jnp.exp(row_max - new_max) + jnp.sum(weights, axis=2))

    max_init = jnp.full((head_count, row_count), masked_value, jnp.float32)
    sum_init = jnp.zeros((head_count, row_count), jnp.float32)
    row_max, row_sum = lax.fori_loop(0, num_blocks, stats_step, (max_init, sum_init))
    row_delta = jnp.sum(grad_out.astype(jnp.float32) * outputs.astype(jnp.float32), axis=2).T

    def grad_step(step_id, state_now):
        query_grad, key_acc, value_acc = state_now
        offset = step_id * block_size
        mask = allowed_fn(offset)[None]
        key_block = lax.dynamic_slice_in_dim(key_rows, offset, block_size, 0)
        value_block = lax.dynamic_slice_in_dim(values, offset, block_size, 0)
        scores = jnp.where(mask, scores_of(queries, key_block), masked_value)
        weights = jnp.where(mask, jnp.exp(scores - row_max[:, :, None]), 0.0)
        probability = weights / row_sum[:, :, None] * live_rows[None, :, None]
        rounded = probability.astype(jnp.bfloat16)
        prob_grad = jnp.einsum(
            "nhd,md->hnm", grad_out, value_block, preferred_element_type=jnp.float32
        )
        score_grad = (probability * (prob_grad - row_delta[:, :, None]) * scaling).astype(
            jnp.bfloat16
        )
        query_grad = query_grad + jnp.einsum(
            "hnm,md->nhd", score_grad, key_block, preferred_element_type=jnp.float32
        )
        key_part = jnp.einsum(
            "hnm,nhd->md", score_grad, queries, preferred_element_type=jnp.float32
        )
        value_part = jnp.einsum(
            "hnm,nhd->md", rounded, grad_out, preferred_element_type=jnp.float32
        )
        key_acc = lax.dynamic_update_slice_in_dim(
            key_acc, lax.dynamic_slice_in_dim(key_acc, offset, block_size, 0) + key_part, offset, 0
        )
        value_acc = lax.dynamic_update_slice_in_dim(
            value_acc,
            lax.dynamic_slice_in_dim(value_acc, offset, block_size, 0) + value_part,
            offset,
            0,
        )
        return (query_grad, key_acc, value_acc)

    query_init = jnp.zeros(queries.shape, jnp.float32)
    return lax.fori_loop(0, num_blocks, grad_step, (query_init, key_grads, value_grads))


def on_device(
    prompt_query,
    prompt_key,
    prompt_value,
    prompt_cotangent,
    prompt_output,
    response_query,
    response_key,
    response_value,
    response_cotangent,
    response_output,
    lengths,
):
    head_dim = prompt_key.shape[1]
    head_count = prompt_query.shape[1] // head_dim
    ctx_count = lax.axis_size("ctx")
    ctx_index = lax.axis_index("ctx")
    sample_index = lax.axis_index("sample")
    full_prompt_keys, full_prompt_values = (
        lax.all_gather(prompt_key, "ctx", axis=0, tiled=True),
        lax.all_gather(prompt_value, "ctx", axis=0, tiled=True),
    )
    own_keys, own_values = (
        lax.all_gather(response_key[0], "ctx", axis=0, tiled=True),
        lax.all_gather(response_value[0], "ctx", axis=0, tiled=True),
    )
    prompt_total = full_prompt_keys.shape[0]
    slot_total = own_keys.shape[0]
    key_rows = jnp.concatenate([full_prompt_keys, own_keys], axis=0)
    value_rows = jnp.concatenate([full_prompt_values, own_values], axis=0)
    block_size = min(512, prompt_total, slot_total)
    empty_grads = jnp.zeros((prompt_total + slot_total, head_dim), jnp.float32)
    local_rows = response_query.shape[1]
    resp_queries = response_query[0].reshape(local_rows, head_count, head_dim)
    resp_grad_out = response_cotangent[0].reshape(local_rows, head_count, head_dim)
    resp_outputs = response_output[0].reshape(local_rows, head_count, head_dim)
    first_row = ctx_index * local_rows
    row_ids = first_row + jnp.arange(local_rows, dtype=jnp.int32)
    length = lengths[0]
    live_rows = (row_ids < length).astype(jnp.float32)
    reach = jnp.minimum(length, first_row + local_rows)
    resp_blocks = jnp.where(
        length > first_row, prompt_total // block_size + (reach + block_size - 1) // block_size, 0
    )

    def response_allowed(offset):
        columns = offset + jnp.arange(block_size, dtype=jnp.int32)
        return (columns[None, :] < prompt_total) | (
            (columns - prompt_total)[None, :] <= row_ids[:, None]
        )

    resp_query_grad, key_grads, value_grads = attend_back(
        resp_queries,
        resp_grad_out,
        resp_outputs,
        key_rows,
        value_rows,
        resp_blocks,
        block_size,
        response_allowed,
        live_rows,
        empty_grads,
        empty_grads,
    )
    prompt_rows = prompt_query.shape[0]
    row_start = (sample_index * ctx_count + ctx_index) * prompt_rows
    prompt_ids = row_start + jnp.arange(prompt_rows, dtype=jnp.int32)
    prompt_blocks = (row_start + prompt_rows + block_size - 1) // block_size

    def prompt_allowed(offset):
        columns = offset + jnp.arange(block_size, dtype=jnp.int32)
        return columns[None, :] <= prompt_ids[:, None]

    prompt_live = jnp.ones((prompt_rows,), jnp.float32)
    prompt_q_grad, key_grads, value_grads = attend_back(
        prompt_query.reshape(prompt_rows, head_count, head_dim),
        prompt_cotangent.reshape(prompt_rows, head_count, head_dim),
        prompt_output.reshape(prompt_rows, head_count, head_dim),
        key_rows,
        value_rows,
        prompt_blocks,
        block_size,
        prompt_allowed,
        prompt_live,
        key_grads,
        value_grads,
    )
    resp_key_sum, resp_value_sum = (
        lax.psum_scatter(
            key_grads[prompt_total:].astype(jnp.bfloat16), "ctx", scatter_dimension=0, tiled=True
        ).astype(jnp.float32),
        lax.psum_scatter(
            value_grads[prompt_total:].astype(jnp.bfloat16), "ctx", scatter_dimension=0, tiled=True
        ).astype(jnp.float32),
    )
    prompt_key_sum, prompt_value_sum = (
        lax.psum_scatter(
            key_grads[:prompt_total], ("sample", "ctx"), scatter_dimension=0, tiled=True
        ),
        lax.psum_scatter(
            value_grads[:prompt_total], ("sample", "ctx"), scatter_dimension=0, tiled=True
        ),
    )
    return (
        prompt_q_grad.reshape(prompt_rows, head_count * head_dim).astype(jnp.bfloat16),
        prompt_key_sum.astype(jnp.bfloat16),
        prompt_value_sum.astype(jnp.bfloat16),
        resp_query_grad.reshape(1, local_rows, head_count * head_dim).astype(jnp.bfloat16),
        resp_key_sum.reshape(1, local_rows, head_dim).astype(jnp.bfloat16),
        resp_value_sum.reshape(1, local_rows, head_dim).astype(jnp.bfloat16),
    )


def solution(mesh):
    placed = (
        P(("sample", "ctx"), None),
        P("ctx", None),
        P("ctx", None),
        P(("sample", "ctx"), None),
        P(("sample", "ctx"), None),
        P("sample", "ctx", None),
        P("sample", "ctx", None),
        P("sample", "ctx", None),
        P("sample", "ctx", None),
        P("sample", "ctx", None),
        P("sample"),
    )
    return jax.shard_map(
        on_device,
        mesh=mesh,
        in_specs=placed,
        out_specs=(
            P(("sample", "ctx"), None),
            P(("sample", "ctx"), None),
            P(("sample", "ctx"), None),
            P("sample", "ctx", None),
            P("sample", "ctx", None),
            P("sample", "ctx", None),
        ),
        check_vma=False,
    )
```

profile of v0, /device:TPU:6, one launch (start us, length us, event | category | flops | bytes accessed | tf_op | source)
XLA Modules:
  0.0 1741.1 jit_solution(11538478113638723174)
XLA Ops:
  9.4 36.0 %all-gather = bf16[1,2048,128]{2,1,0:T(8,128)(2,1)S(1)} all-gather(bf16[1,256,128]{2,1,0:T(8,128)(2,1)} %param.25), channel_id=2, replica_groups=mesh['sample'=16,'ctx'=8] {'ctx'}, dimensions={1}, use_global_device_ids=true | all-gather | bytes 589824 | tf_op jit(solution)/shard_map/all_gather | solution.py:111
  46.9 35.8 %all-gather.1 = bf16[1,2048,128]{2,1,0:T(8,128)(2,1)S(1)} all-gather(bf16[1,256,128]{2,1,0:T(8,128)(2,1)} %param.26), channel_id=3, replica_groups=mesh['sample'=16,'ctx'=8] {'ctx'}, dimensions={1}, use_global_device_ids=true | all-gather | bytes 589824 | tf_op jit(solution)/shard_map/all_gather | solution.py:112
  83.9 2.5 pad_maximum_fusion
  86.4 27.1 %while.61 = (s32[]{:T(128)}, f32[8,256]{1,0:T(8,128)S(1)}, f32[8,256]{1,0:T(8,128)S(1)}, s32[]{:T(128)}, bf16[6144,128]{1,0:T(8,128)(2,1)}, /*index=5*/bf16[256,...) while((s32[]{:T(128)}, f32[8,256]{1,0:T(8,128)S(1)}, ...), condition=%wide.region_3.4_spmd.clone, body=%wide.region_0.3_spmd.clone.sunk | while | flops 277092608 | bytes 9551019 | solution.py:45
  113.6 2.6 pad_maximum_fusion.1
  120.0 100.6 %while.64 = (s32[]{:T(128)}, f32[256,8,128]{0,2,1:T(8,128)S(1)}, f32[6144,128]{1,0:T(8,128)}, f32[6144,128]{1,0:T(8,128)}, s32[]{:T(128)}, /*index=5*/bf16[6144,...) while((s32[]{:T(128)}, f32[256,8,128]{0,2,1:T(8,128)S(1)}, ...), condition=%wide.region_6.7_spmd.clone.clone, body=%wide.region_5.6_spmd.clone.clone.sunk | while | flops 1354370048 | bytes 24806652 | solution.py:85
  125.0 2.4 fusion.172
  127.4 2.4 fusion.173
  136.1 2.4 fusion.172
  138.5 2.4 fusion.173
  147.3 2.4 fusion.172
  149.7 2.4 fusion.173
  158.4 2.4 fusion.172
  160.9 2.4 fusion.173
  169.6 2.4 fusion.172
  172.0 2.4 fusion.173
  180.8 2.4 fusion.172
  183.2 2.4 fusion.173
  192.0 2.4 fusion.172
  194.4 2.4 fusion.173
  203.1 2.4 fusion.172
  205.5 2.4 fusion.173
  214.3 2.5 fusion.172
  216.8 2.4 fusion.173
  220.6 11.4 while.62
  232.0 52.6 %while.63 = (s32[]{:T(128)}, f32[32,8,128]{2,0,1:T(8,128)S(1)}, f32[6144,128]{1,0:T(8,128)}, f32[6144,128]{1,0:T(8,128)}, s32[]{:T(128)}, /*index=5*/bf16[6144,1...) while((s32[]{:T(128)}, f32[32,8,128]{2,0,1:T(8,128)S(1)}, ...), condition=%wide.region_13.14_spmd.clone, body=%wide.region_12.13_spmd.clone.sunk | while | flops 169263648 | bytes 4365799 | solution.py:85
  284.7 3.1 slice.14
  287.8 3.1 slice.15
  297.0 603.3 %reduce-scatter.5.cloned.1.call-done = f32[32,128]{1,0:T(8,128)} async-done(((f32[4096,128]{1,0:T(8,128)}), f32[32,128]{1,0:T(8,128)}) %reduce-scatter.5.cloned.1.call-update) | async-done | bytes 16400 | tf_op jit(solution)/shard_map/reduce_scatter | solution.py:184
  901.5 636.6 %reduce-scatter.7.cloned.1.call-done = f32[32,128]{1,0:T(8,128)} async-done(((f32[4096,128]{1,0:T(8,128)}), f32[32,128]{1,0:T(8,128)}) %reduce-scatter.7.cloned.1.call-update) | async-done | bytes 16400 | tf_op jit(solution)/shard_map/reduce_scatter | solution.py:187
  1539.4 120.7 %reduce-scatter.11.cloned.1.call-done = bf16[256,128]{1,0:T(8,128)(2,1)} async-done(((bf16[2048,128]{1,0:T(8,128)(2,1)}), bf16[256,128]{1,0:T(8,128)(2,1)}) %reduce-scatter.11.cloned.1.call-update) | async-done | bytes 65552 | tf_op jit(solution)/shard_map/reduce_scatter | solution.py:179
  1660.1 74.2 %reduce-scatter.9.cloned.1.call-done = bf16[256,128]{1,0:T(8,128)(2,1)} async-done(((bf16[2048,128]{1,0:T(8,128)(2,1)}), bf16[256,128]{1,0:T(8,128)(2,1)}) %reduce-scatter.9.cloned.1.call-update) | async-done | bytes 65552 | tf_op jit(solution)/shard_map/reduce_scatter | solution.py:176
  (316 shorter events, 162.5 us)
Async XLA Ops:
  7.2 76.5 %copy-start = (bf16[32,1024]{1,0:T(8,128)(2,1)S(1)}, bf16[32,1024]{1,0:T(8,128)(2,1)}, u32[]{:S(2)}) copy-start(bf16[32,1024]{1,0:T(8,128)(2,1)} %param.19) | copy-start | bytes 196612
  7.2 75.6 %copy-start.1 = (bf16[1,256,1024]{2,1,0:T(8,128)(2,1)S(1)}, bf16[1,256,1024]{2,1,0:T(8,128)(2,1)}, u32[]{:S(2)}) copy-start(bf16[1,256,1024]{2,1,0:T(8,128)(2,1)} %param.27) | copy-start | bytes 1572868
  7.2 75.8 %copy-start.2 = (bf16[1,256,1024]{2,1,0:T(8,128)(2,1)S(1)}, bf16[1,256,1024]{2,1,0:T(8,128)(2,1)}, u32[]{:S(2)}) copy-start(bf16[1,256,1024]{2,1,0:T(8,128)(2,1)} %param.28) | copy-start | bytes 1572868
  7.2 76.7 %all-gather.5.cloned.1.call-start = ((), (), s32[]{:S(2)}) async-start(), calls=%async_computation.4 | async-start | bytes 1179648 | tf_op jit(solution)/shard_map/all_gather | solution.py:107
  7.9 105.6 %all-gather.7.cloned.1.call-start = ((), (), s32[]{:S(2)}) async-start(), calls=%async_computation.5 | async-start | bytes 1179648 | tf_op jit(solution)/shard_map/all_gather | solution.py:108
  8.7 891.5 %reduce-scatter.5.cloned.1.call-start = ((), (), s32[]{:S(2)}) async-start(), calls=%async_computation.6 | async-start | bytes 2113536 | tf_op jit(solution)/shard_map/reduce_scatter | solution.py:184
  46.6 37.0 %copy-start.4 = (bf16[32,1024]{1,0:T(8,128)(2,1)S(1)}, bf16[32,1024]{1,0:T(8,128)(2,1)}, u32[]{:S(2)}) copy-start(bf16[32,1024]{1,0:T(8,128)(2,1)} %param.23) | copy-start | bytes 196612
  46.7 37.0 %copy-start.3 = (bf16[32,1024]{1,0:T(8,128)(2,1)S(1)}, bf16[32,1024]{1,0:T(8,128)(2,1)}, u32[]{:S(2)}) copy-start(bf16[32,1024]{1,0:T(8,128)(2,1)} %param.22) | copy-start | bytes 196612
  287.8 1250.3 %reduce-scatter.7.cloned.1.call-start = ((), (), s32[]{:S(2)}) async-start(), calls=%async_computation.7 | async-start | bytes 2113536 | tf_op jit(solution)/shard_map/reduce_scatter | solution.py:187
  290.9 1369.1 %reduce-scatter.11.cloned.1.call-start = ((), (), s32[]{:S(2)}) async-start(), calls=%async_computation.9 | async-start | bytes 589824 | tf_op jit(solution)/shard_map/reduce_scatter | solution.py:179
  293.1 1441.2 %reduce-scatter.9.cloned.1.call-start = ((), (), s32[]{:S(2)}) async-start(), calls=%async_computation.8 | async-start | bytes 589824 | tf_op jit(solution)/shard_map/reduce_scatter | solution.py:176
Sparse Core Ops, SparseCore 0:
  10.4 52.4 all-gather.4
  65.2 45.8 all-gather.6
  287.9 612.3 reduce-scatter.4
  902.5 635.5 reduce-scatter.6
  1542.1 117.9 reduce-scatter.10
  1664.5 69.7 reduce-scatter.8
where the time goes:
time: 1740 us
  waiting for transfers between devices  1440 us (83%)
  matrix products  167 us (10%)
  blocking collectives  71.8 us (4%)
  other arithmetic  30.6 us (2%)
  local copies, waits for them, and re-layouts  17.6 us (1%)
    reduce_scatter x1, waiting for transfers between devices, on_device(): lax.psum_scatter(value_grads[:prompt_total], ('sample', 'ctx'), scatter_d...  637 us
    reduce_scatter x1, waiting for transfers between devices, on_device(): lax.psum_scatter(key_grads[:prompt_total], ('sample', 'ctx'), scatter_dim...  603 us
    reduce_scatter x1, waiting for transfers between devices, on_device(): lax.psum_scatter(value_grads[prompt_total:].astype(jnp.bfloat16), 'ctx',...  121 us
    reduce_scatter x1, waiting for transfers between devices, on_device(): lax.psum_scatter(key_grads[prompt_total:].astype(jnp.bfloat16), 'ctx', sc...  74.2 us
    dot_general x32, matrix products, scores_of(): jnp.einsum('nhd,md->hnm', queries, key_rows, preferred_element_type=jnp.f...  53.5 us
    all_gather x1, blocking collectives, on_device(): lax.all_gather(response_key[0], 'ctx', axis=0, tiled=True)  36 us
    all_gather x1, blocking collectives, on_device(): lax.all_gather(response_value[0], 'ctx', axis=0, tiled=True)  35.8 us
    dot_general x16, matrix products, grad_step(): jnp.einsum('hnm,nhd->md', score_grad, queries, preferred_element_type=jnp...  35.3 us
  transfers between devices with their start and end apart: 6, of which 4 were waited for; matrix products, arithmetic and copies ran while one was open for 2% of the time, Pallas kernels for 0%

commit v1 on v0

v1 whole, which is shorter than its diff:
```python
import functools

import jax
import jax.numpy as jnp
from jax import lax
from jax.experimental import pallas as pl
from jax.experimental.pallas import tpu as pltpu
from jax.sharding import PartitionSpec as P

f32 = jnp.float32
bf16 = jnp.bfloat16
LOG2E = 1.4426950408889634
MASKED = -1e30
NT = (((1,), (1,)), ((), ()))
NN = (((1,), (0,)), ((), ()))
TN = (((0,), (0,)), ((), ()))


def dot(a, b, dims):
    return lax.dot_general(a, b, dims, preferred_element_type=f32)


def kernel(
    NS, NC, H, KC, PR,
    pq_ref, pk_ref, pv_ref, pg_ref, po_ref, rq_ref, rk_ref, rv_ref, rg_ref, ro_ref, len_ref,
    dpq_ref, dpk_ref, dpv_ref, drq_ref, drk_ref, drv_ref,
    q, g, qp, gp, kall, vall, E, Ep, SA, SB, PB, GB, PBp, GBp,
    M2, S, Mj, Mt, Inv, D, M2p, Sp, Mjp, Dp, dqt, dqtp, DKV,
    keep, sibs, sibr, xs, xr, cs, cr, ownf, os_, or_,
    ks_s, ks_r, kf_s, kf_r, vs_s, vs_r, vf_s, vf_r, ok_s, ok_r, ov_s, ov_r,
    sib_s, sib_r, x_s, x_r, c_s, c_r, o_s, o_r,
):
    DH = 128
    RC = KC // 2
    NR = RC * H
    NPC = PR * H
    NP = NS // 2
    Y = NC // 2
    scaling = DH**-0.5
    C = scaling * LOG2E
    s_id = lax.axis_index("sample")
    c = lax.axis_index("ctx")
    core, zl, x = s_id % 2, (s_id // 2) % 2, s_id // 4
    zh, y = c % 2, c // 2
    pair = s_id // 2
    row0 = (s_id * NC + c) * PR
    jd = row0 // KC
    half = pl.ds(core * RC, RC)
    other = pl.ds((1 - core) * RC, RC)

    def dev(s, ct):
        return {"sample": s, "ctx": ct}

    sibling = dev(s_id + 1 - 2 * core, c)

    def rcopy(src, dst, send, recv, device):
        return pltpu.make_async_remote_copy(
            src_ref=src, dst_ref=dst, send_sem=send, recv_sem=recv,
            device_id=device, device_id_type=pl.DeviceIdType.MESH,
        )

    def g_dev(r):
        dy, dz = r // 2, r % 2
        zl2 = zl + dz - 2 * zl * dz
        zh2 = zh + dz - 2 * zh * dz
        return dev(x * 4 + zl2 * 2 + core, ((y + dy) % Y) * 2 + zh2)

    def g_src(r):
        dy, dz = r // 2, r % 2
        return ((y + Y - dy) % Y) * 2 + zh + dz - 2 * zh * dz

    def send_half(buf, ss, rs, r):
        return rcopy(buf.at[c, half], buf.at[c, half], ss.at[r], rs.at[r], g_dev(r))

    def got_half(buf, ss, rs, r):
        i = g_src(r)
        return rcopy(buf.at[i, half], buf.at[i, half], ss.at[r], rs.at[r], sibling)

    def got_other(buf, ss, rs, r):
        i = g_src(r)
        return rcopy(buf.at[i, other], buf.at[i, other], ss.at[r], rs.at[r], sibling)

    def own_at(buf, i):
        return buf.at[NC + i // 2, pl.ds((i % 2) * RC, RC)]

    def own_send(buf, ss, rs, to):
        return rcopy(own_at(buf, c), own_at(buf, c), ss.at[to], rs.at[c], dev(s_id, to))

    def own_got(buf, ss, rs, i):
        return rcopy(own_at(buf, i), own_at(buf, i), ss.at[i], rs.at[i], sibling)

    barrier = pltpu.get_barrier_semaphore()

    def greet(device):
        pl.semaphore_signal(
            barrier, inc=1, device_id=device, device_id_type=pl.DeviceIdType.MESH
        )

    greet(sibling)
    for t in range(1, NC):
        greet(dev(s_id, (c + t) % NC))
    for r in range(1, NC, 2):
        greet(g_dev(r))
    for t in range(1, NP):
        greet(dev(((pair + t) % NP) * 2 + core, c))

    kall[c] = pk_ref[...]
    vall[c] = pv_ref[...]
    kall[NC + c // 2, pl.ds((c % 2) * RC, RC)] = rk_ref[0]
    vall[NC + c // 2, pl.ds((c % 2) * RC, RC)] = rv_ref[0]

    @pl.when(c % 2 == 0)
    def _():
        kall[NC + c // 2, RC:] = jnp.zeros((RC, DH), bf16)
        vall[NC + c // 2, RC:] = jnp.zeros((RC, DH), bf16)

    pl.semaphore_wait(barrier, 1 + (NC - 1) + NC // 2 + (NP - 1))

    for r in range(1, NC):
        send_half(kall, ks_s, ks_r, r).start()

    @pl.loop(c + 1, NC)
    def _(to):
        own_send(kall, ok_s, ok_r, to).start()

    for r in range(1, NC):
        send_half(vall, vs_s, vs_r, r).start()

    @pl.loop(c + 1, NC)
    def _(to):
        own_send(vall, ov_s, ov_r, to).start()

    ones = jnp.ones((8, DH), bf16)

    def delta(gr, o):
        prod = gr.astype(f32) * o.astype(f32)
        hi = prod.astype(bf16)
        lo = (prod - hi.astype(f32)).astype(bf16)
        return dot(ones, hi, NT) + dot(ones, lo, NT)

    for h in range(H):
        cols = slice(h * DH, (h + 1) * DH)
        rows = slice(h * RC, (h + 1) * RC)
        q[rows] = rq_ref[0, :, cols]
        g[rows] = rg_ref[0, :, cols]
        qp[h * PR : (h + 1) * PR] = pq_ref[:, cols]
        gp[h * PR : (h + 1) * PR] = pg_ref[:, cols]
        D[:, rows] = delta(rg_ref[0, :, cols], ro_ref[0, :, cols])
    prod_o = jnp.concatenate([po_ref[:, h * DH : (h + 1) * DH] for h in range(H)], axis=0)
    Dp[...] = delta(gp[...], prod_o)
    M2[...] = jnp.full_like(M2, MASKED)
    S[...] = jnp.zeros_like(S)
    M2p[...] = jnp.full_like(M2p, MASKED)
    Sp[...] = jnp.zeros_like(Sp)
    dqt[...] = jnp.zeros_like(dqt)
    dqtp[...] = jnp.zeros_like(dqtp)

    L = NC + c // 2

    def id_of(p):
        own = p // NC
        return g_src(p % NC) * (1 - own) + p * own

    def first(i_id, buf, h):
        cols = slice(h * RC, (h + 1) * RC)
        s = dot(kall[i_id], q[cols], NT)
        buf[:, cols] = s
        M2[0, :, cols] = jnp.maximum(
            M2[0, :, cols], jnp.max(s.reshape(KC // 8, 8, RC), axis=0)
        )

    def second(i_id, buf, h):
        cols = slice(h * RC, (h + 1) * RC)
        s = buf[:, cols].reshape(KC // 8, 8, RC)
        new, old = M2[1, :, cols], M2[2, :, cols]
        e = jnp.exp2((s - new) * C)
        S[:, cols] = S[:, cols] * jnp.exp2((old - new) * C) + jnp.sum(e, axis=0)
        E[pl.ds(pl.multiple_of(i_id * KC, KC), KC), cols] = e.reshape(KC, RC).astype(bf16)

    def rotate(i_id):
        M2[2] = M2[1]
        M2[1] = M2[0]
        Mj[i_id] = M2[0]

    def forward_k(p):
        @pl.when(p < NC)
        def _():
            got_half(kall, ks_s, ks_r, p).wait_recv()
            i = g_src(p)
            rcopy(kall.at[i, half], kall.at[i, half], kf_s.at[p], kf_r.at[p], sibling).start()

    def ready(p):
        forward_k(p + 1)

        @pl.when(p < NC)
        def _():
            got_other(kall, kf_s, kf_r, p).wait_recv()

        @pl.when((p >= NC) & (p < L))
        def _():
            own_got(kall, ok_s, ok_r, 2 * (p - NC)).wait_recv()
            own_got(kall, ok_s, ok_r, 2 * (p - NC) + 1).wait_recv()

    for h in range(H):
        first(c, SA, h)
    rotate(c)
    forward_k(1)

    @pl.loop(0, (L + 1) // 2)
    def _(t):
        p = 2 * t
        ready(p + 1)
        a, b = id_of(p), id_of(jnp.minimum(p + 1, L - 1))
        for h in range(H):
            first(b, SB, h)
            second(a, SA, h)
        rotate(b)

        @pl.when(p + 1 < L)
        def _():
            ready(p + 2)
            d = id_of(jnp.minimum(p + 2, L - 1))
            for h in range(H):
                first(d, SA, h)
                second(b, SB, h)
            rotate(d)

    @pl.when(c % 2 == 1)
    def _():
        own_got(kall, ok_s, ok_r, c - 1).wait_recv()

    dg = NC + c // 2
    key_at = lax.broadcasted_iota(jnp.int32, (KC, RC), 0)
    row_at = lax.broadcasted_iota(jnp.int32, (KC, RC), 1) + (c % 2) * RC
    seen = key_at <= row_at
    for h in range(H):
        cols = slice(h * RC, (h + 1) * RC)
        s = jnp.where(seen, dot(kall[dg], q[cols], NT), MASKED).reshape(KC // 8, 8, RC)
        old = M2[1, :, cols]
        new = jnp.maximum(old, jnp.max(s, axis=0))
        e = jnp.exp2((s - new) * C)
        S[:, cols] = S[:, cols] * jnp.exp2((old - new) * C) + jnp.sum(e, axis=0)
        E[pl.ds(pl.multiple_of(dg * KC, KC), KC), cols] = e.reshape(KC, RC).astype(bf16)
        Mj[dg, :, cols] = new
        M2[0, :, cols] = new

    for r in range(1, NC):
        got_half(vall, vs_s, vs_r, r).wait_recv()
        i = g_src(r)
        rcopy(vall.at[i, half], vall.at[i, half], vf_s.at[r], vf_r.at[r], sibling).start()

    @pl.loop(0, jd + 1)
    def _(j):
        s = dot(kall[j], qp[...], NT)
        keys = j * KC + lax.broadcasted_iota(jnp.int32, (KC, NPC), 0)
        rows = row0 + lax.broadcasted_iota(jnp.int32, (KC, NPC), 1) % PR
        ok = (keys <= rows).reshape(KC // 8, 8, NPC)
        s = jnp.where(ok, s.reshape(KC // 8, 8, NPC), MASKED)
        old = M2p[...]
        new = jnp.maximum(old, jnp.max(s, axis=0))
        e = jnp.where(ok, jnp.exp2((s - new) * C), 0.0)
        Sp[...] = Sp[...] * jnp.exp2((old - new) * C) + jnp.sum(e, axis=0)
        Ep[pl.ds(pl.multiple_of(j * KC, KC), KC)] = e.reshape(KC, NPC).astype(bf16)
        Mjp[j] = new
        M2p[...] = new

    length = len_ref[0]
    live = (c * RC + lax.broadcasted_iota(jnp.int32, (1, NR), 1) % RC) < length
    m = M2[0]
    mt = jnp.max(m, axis=0, keepdims=True)
    st = jnp.sum(S[...] * jnp.exp2((m - mt) * C), axis=0, keepdims=True)
    Mt[...] = mt
    Inv[...] = jnp.where(live, 1.0 / st, 0.0)
    mp = M2p[...]
    mpt = jnp.max(mp, axis=0, keepdims=True)
    invp = 1.0 / jnp.sum(Sp[...] * jnp.exp2((mp - mpt) * C), axis=0, keepdims=True)

    def grads(i_id):
        base = pl.ds(pl.multiple_of(i_id * KC, KC), KC)
        for h in range(H):
            cols = slice(h * RC, (h + 1) * RC)
            dp = dot(vall[i_id], g[cols], NT)
            w = jnp.exp2((Mj[i_id, :, cols] - Mt[:, cols]) * C) * Inv[:, cols]
            p = (E[base, cols].astype(f32).reshape(KC // 8, 8, RC) * w).astype(bf16)
            p = p.reshape(KC, RC)
            PB[:, cols] = p
            GB[:, cols] = (dp - D[0:1, cols]).astype(bf16) * p
        DKV[1] = dot(PB[...], g[...], NN)
        DKV[0] = dot(GB[...], q[...], NN)
        for h in range(H):
            cols = slice(h * RC, (h + 1) * RC)
            dqt[h] += dot(kall[i_id], GB[:, cols], TN)

    def grads_prompt(j):
        base = pl.ds(pl.multiple_of(j * KC, KC), KC)
        dp = dot(vall[j], gp[...], NT)
        w = jnp.exp2((Mjp[j] - mpt) * C) * invp
        p = (Ep[base].astype(f32).reshape(KC // 8, 8, NPC) * w).astype(bf16).reshape(KC, NPC)
        ds = (dp - Dp[0:1]).astype(bf16) * p
        DKV[1] += dot(p, gp[...], NN)
        DKV[0] += dot(ds, qp[...], NN)
        dqtp[...] += dot(kall[j], ds, TN)

    @pl.loop(0, c)
    def _(i):
        own_got(vall, ov_s, ov_r, i).wait_recv()

    def own_grad_send(to):
        return rcopy(os_.at[to], or_.at[c], o_s.at[to], o_r.at[c], dev(s_id, to))

    @pl.loop(0, c // 2 + 1)
    def _(jo):
        grads(NC + jo)
        for hf in range(2):
            to = 2 * jo + hf
            part = DKV[:, hf * RC : (hf + 1) * RC]

            @pl.when(to == c)
            def _():
                ownf[...] = part

            @pl.when(to < c)
            def _():
                os_[to] = jnp.stack([part[0] * scaling, part[1]]).astype(bf16)
                own_grad_send(to).start()

    for r in range(1, NC):
        got_other(vall, vf_s, vf_r, r).wait_recv()

    def sib_copy(i):
        return rcopy(sibs.at[i], sibr.at[i], sib_s.at[i], sib_r.at[i], sibling)

    def x_send(i):
        to = ((pair + 1 + i) % NP) * 2 + core
        return rcopy(xs.at[i], xr.at[pair], x_s.at[i], x_r.at[pair], dev(to, c))

    @pl.loop(0, NP)
    def _(i):
        j = (pair + 1 + i) % NP
        grads(j)

        @pl.when(j <= jd)
        def _():
            grads_prompt(j)

        keep[i, 0] = DKV[0, half] * scaling
        keep[i, 1] = DKV[1, half]
        sibs[i, 0] = (DKV[0, other] * scaling).astype(bf16)
        sibs[i, 1] = DKV[1, other].astype(bf16)
        sib_copy(i).start()

        @pl.when(i >= 1)
        def _():
            sib_copy(i - 1).wait_recv()
            xs[i - 1] = (keep[i - 1] + sibr[i - 1].astype(f32)).astype(bf16)
            x_send(i - 1).start()

    for h in range(H):
        cols = slice(h * DH, (h + 1) * DH)
        drq_ref[0, :, cols] = (dqt[h].T * scaling).astype(bf16)
    dqp = (dqtp[...].T * scaling).astype(bf16)
    for h in range(H):
        dpq_ref[:, h * DH : (h + 1) * DH] = dqp[h * PR : (h + 1) * PR]

    sib_copy(NP - 1).wait_recv()
    total = keep[NP - 1] + sibr[NP - 1].astype(f32)
    for t in range(1, NP):
        k = (pair + t) % NP
        rcopy(xr.at[k], xr.at[k], x_s.at[t - 1], x_r.at[k], sibling).wait_recv()
        total = total + xr[k].astype(f32)
    keep[NP - 1] = total

    def c_send(t):
        to = (c + t) % NC
        return rcopy(cs.at[t], cr.at[c], c_s.at[t], c_r.at[c], dev(s_id, to))

    for t in range(1, NC):
        to = (c + t) % NC
        cs[t] = keep[NP - 1, :, pl.ds(to * PR, PR)].astype(bf16)
        c_send(t).start()

    ownf[0] = ownf[0] * scaling

    @pl.loop(c + 1, NC)
    def _(i):
        rcopy(or_.at[i], or_.at[i], o_s.at[i], o_r.at[i], sibling).wait_recv()
        ownf[...] += or_[i].astype(f32)

    drk_ref[0] = ownf[0].astype(bf16)
    drv_ref[0] = ownf[1].astype(bf16)

    total = keep[NP - 1, :, pl.ds(c * PR, PR)]
    for t in range(1, NC):
        k = (c + t) % NC
        rcopy(cr.at[k], cr.at[k], c_s.at[t], c_r.at[k], sibling).wait_recv()
        total = total + cr[k].astype(f32)
    dpk_ref[...] = total[0].astype(bf16)
    dpv_ref[...] = total[1].astype(bf16)

    for r in range(1, NC):
        send_half(kall, ks_s, ks_r, r).wait_send()
        send_half(vall, vs_s, vs_r, r).wait_send()
        got_half(kall, kf_s, kf_r, r).wait_send()
        got_half(vall, vf_s, vf_r, r).wait_send()
        c_send(r).wait_send()

    @pl.loop(c + 1, NC)
    def _(to):
        own_send(kall, ok_s, ok_r, to).wait_send()
        own_send(vall, ov_s, ov_r, to).wait_send()

    @pl.loop(0, c)
    def _(to):
        own_grad_send(to).wait_send()

    for i in range(NP):
        sib_copy(i).wait_send()
    for i in range(NP - 1):
        x_send(i).wait_send()


def on_device(NS, NC, *args):
    pq, pk = args[0], args[1]
    rq = args[5]
    DH = pk.shape[1]
    H = pq.shape[1] // DH
    KC, PR, RC = pk.shape[0], pq.shape[0], rq.shape[1]
    NR, NPC, NP, NK = RC * H, PR * H, NS // 2, NC + NC // 2
    vm = pltpu.VMEM
    dma = pltpu.SemaphoreType.DMA
    sds = jax.ShapeDtypeStruct
    scratch = [
        vm((NR, DH), bf16), vm((NR, DH), bf16), vm((NPC, DH), bf16), vm((NPC, DH), bf16),
        vm((NK, KC, DH), bf16), vm((NK, KC, DH), bf16),
        vm((NK * KC, NR), bf16), vm((NC * KC, NPC), bf16),
        vm((KC, NR), f32), vm((KC, NR), f32), vm((KC, NR), bf16), vm((KC, NR), bf16),
        vm((8, 128), bf16), vm((8, 128), bf16),
        vm((3, 8, NR), f32), vm((8, NR), f32), vm((NK, 8, NR), f32), vm((1, NR), f32),
        vm((1, NR), f32), vm((8, NR), f32),
        vm((8, NPC), f32), vm((8, NPC), f32), vm((NC, 8, NPC), f32), vm((8, NPC), f32),
        vm((H, DH, RC), f32), vm((DH, NPC), f32), vm((2, KC, DH), f32),
        vm((NP, 2, RC, DH), f32), vm((NP, 2, RC, DH), bf16), vm((NP, 2, RC, DH), bf16),
        vm((NP, 2, RC, DH), bf16), vm((NP, 2, RC, DH), bf16),
        vm((NC, 2, PR, DH), bf16), vm((NC, 2, PR, DH), bf16),
        vm((2, RC, DH), f32), vm((NC, 2, RC, DH), bf16), vm((NC, 2, RC, DH), bf16),
    ]
    scratch += [dma((NC,))] * 12 + [dma((NP,))] * 4 + [dma((NC,))] * 4
    vspec = pl.BlockSpec(memory_space=pltpu.VMEM)
    return pl.pallas_call(
        functools.partial(kernel, NS, NC, H, KC, PR),
        out_shape=(
            sds((PR, H * DH), bf16), sds((PR, DH), bf16), sds((PR, DH), bf16),
            sds((1, RC, H * DH), bf16), sds((1, RC, DH), bf16), sds((1, RC, DH), bf16),
        ),
        in_specs=[vspec] * 10 + [pl.BlockSpec(memory_space=pltpu.SMEM)],
        out_specs=[vspec] * 6,
        scratch_shapes=scratch,
        compiler_params=pltpu.CompilerParams(
            collective_id=0, has_side_effects=True, vmem_limit_bytes=62 * 2**20
        ),
    )(*args)


def solution(mesh):
    placed = (
        P(("sample", "ctx"), None),
        P("ctx", None),
        P("ctx", None),
        P(("sample", "ctx"), None),
        P(("sample", "ctx"), None),
        P("sample", "ctx", None),
        P("sample", "ctx", None),
        P("sample", "ctx", None),
        P("sample", "ctx", None),
        P("sample", "ctx", None),
        P("sample"),
    )
    return jax.shard_map(
        functools.partial(on_device, mesh.shape["sample"], mesh.shape["ctx"]),
        mesh=mesh,
        in_specs=placed,
        out_specs=(
            P(("sample", "ctx"), None),
            P(("sample", "ctx"), None),
            P(("sample", "ctx"), None),
            P("sample", "ctx", None),
            P("sample", "ctx", None),
            P("sample", "ctx", None),
        ),
        check_vma=False,
    )
```

time: 1740 us -> 99.7 us (0.06)
  waiting for transfers between devices: 1440 us -> 0 us
  matrix products: 167 us -> 0 us
  Pallas kernels: 0 us -> 91.9 us
  blocking collectives: 71.8 us -> 0 us
  other arithmetic: 30.6 us -> 0 us
    reduce_scatter x4 -> x0, waiting for transfers between devices: 1430 us -> none  [the longest x1 637 us: on_device(): lax.psum_scatter(value_grads[:prompt_total], ('sample', 'ctx'), scatter_d...]
    dot_general x96 -> x0, matrix products: 167 us -> none  [the longest x32 53.5 us: scores_of(): jnp.einsum('nhd,md->hnm', queries, key_rows, preferred_element_type=jnp.f...]
    pallas_call x0 -> x1, Pallas kernels: none -> 91.9 us  [on_device(): pl.pallas_call(functools.partial(kernel, NS, NC, H, KC, PR), out_shape=(s...]
    all_gather x2 -> x0, blocking collectives: 71.8 us -> none  [the longest x1 36 us: on_device(): lax.all_gather(response_key[0], 'ctx', axis=0, tiled=True)]
  transfers between devices with their start and end apart: 6 -> 0, of which waited for: 4 -> 0; matrix products, arithmetic and copies ran while one was open for 2% -> 0% of each run, Pallas kernels for 0% -> 0%
where the time goes in v1:
time: 99.7 us; the launch traced here: 99.3 us
  Pallas kernels  91.9 us (92%)
  local copies, waits for them, and re-layouts  6.18 us (6%)
  between operations  1.3 us (1%)
    pallas_call x1, Pallas kernels, on_device(): pl.pallas_call(functools.partial(kernel, NS, NC, H, KC, PR), out_shape=(s...  91.9 us
    unnamed x14, local copies, waits for them, and re-layouts  6.18 us

profile of v1, /device:TPU:6, one launch (start us, length us, event | category | flops | bytes accessed | tf_op | source)
XLA Modules:
  0.0 99.3 jit_solution(13668532928334288580)
XLA Ops:
  1.3 91.9 %shard_map.154 = (bf16[32,1024]{1,0:T(8,128)(2,1)}, bf16[32,128]{1,0:T(8,128)(2,1)}, bf16[32,128]{1,0:T(8,128)(2,1)}, bf16[1,256,1024]{2,1,0:T(8,128)(2,1)}, bf1...) custom-call(bf16[32,1024]{1,0:T(8,128)(2,1)} %pq_ref.1, bf16[512,128]{1,0:T(8,128)(2,1)} %pk_ref.1, ...), custom_call_target="tpu_custom_call" | custom-call | tf_op jit(solution)/shard_map/pallas_call | solution.py:449
  93.2 0.0 copy-start.3
  93.2 1.5 %copy.24 = bf16[32,1024]{1,0:T(8,128)(2,1)} copy(bf16[32,1024]{1,0:T(8,128)(2,1)} %get-tuple-element.12) | data formatting | bytes 131072
  94.6 0.0 copy-done.3
  94.7 0.0 copy-start.2
  94.7 0.6 copy.25
  95.3 0.1 copy-done.2
  95.4 0.6 copy.26
  96.0 0.0 copy-start.1
  96.0 1.9 %copy.27 = bf16[1,256,1024]{2,1,0:T(8,128)(2,1)} copy(bf16[1,256,1024]{2,1,0:T(8,128)(2,1)} %get-tuple-element.15) | data formatting | bytes 1048576
  97.9 0.0 copy-done.1
  97.9 0.0 copy-start
  97.9 0.6 copy.28
  98.5 0.2 copy-done
  98.7 0.6 copy.29
Async XLA Ops:
  93.2 1.5 %copy-start.3 = (bf16[32,128]{1,0:T(8,128)(2,1)S(1)}, bf16[32,128]{1,0:T(8,128)(2,1)}, u32[]{:S(2)}) copy-start(bf16[32,128]{1,0:T(8,128)(2,1)} %get-tuple-element.13) | copy-start | bytes 24580
  94.7 0.7 copy-start.2
  96.0 1.9 %copy-start.1 = (bf16[1,256,128]{2,1,0:T(8,128)(2,1)S(1)}, bf16[1,256,128]{2,1,0:T(8,128)(2,1)}, u32[]{:S(2)}) copy-start(bf16[1,256,128]{2,1,0:T(8,128)(2,1)} %get-tuple-element.16) | copy-start | bytes 196612
  97.9 0.9 copy-start

commit v2 on v1

v2 whole, which is shorter than its diff:
```python
import functools

import jax
import jax.numpy as jnp
from jax import lax
from jax.experimental import pallas as pl
from jax.experimental.pallas import tpu as pltpu
from jax.sharding import PartitionSpec as P

f32 = jnp.float32
bf16 = jnp.bfloat16
LOG2E = 1.4426950408889634
MASKED = -1e30
NT = (((1,), (1,)), ((), ()))
NN = (((1,), (0,)), ((), ()))
TN = (((0,), (0,)), ((), ()))


def dot(a, b, dims):
    return lax.dot_general(a, b, dims, preferred_element_type=f32)


def kernel(
    NS, NC, H, KC, PR,
    pq_ref, pk_ref, pv_ref, pg_ref, po_ref, rq_ref, rk_ref, rv_ref, rg_ref, ro_ref, len_ref,
    dpq_ref, dpk_ref, dpv_ref, drq_ref, drk_ref, drv_ref,
    q, g, qp, gp, kall, vall, E, Ep, SA, SB, PB, GB, PBp, GBp,
    M2, S, Mj, Mt, Inv, D, M2p, Sp, Mjp, Dp, dqt, dqtp, DKV,
    keep, sibs, sibr, xs, xr, cs, cr, own_keep, os_, oy, oyr,
    ks_s, ks_r, kf_s, kf_r, vs_s, vs_r, ok_s, ok_r, oz_s, ov_s, ov_r, ow_s,
    vx_s, vx_r, vf_s, vf_r,
    sib_s, sib_r, x_s, x_r, c_s, c_r, o_s, o_r, oy_s, oy_r,
):
    DH = 128
    RC = KC // 2
    NR = RC * H
    NPC = PR * H
    NP = NS // 2
    X = NS // 4
    Y = NC // 2
    EW = KC // (2 * X)
    scaling = DH**-0.5
    C = scaling * LOG2E
    s_id = lax.axis_index("sample")
    c = lax.axis_index("ctx")
    core, zl, x = s_id % 2, (s_id // 2) % 2, s_id // 4
    zh, y = c % 2, c // 2
    pair = s_id // 2
    row0 = (s_id * NC + c) * PR
    jd = row0 // KC
    half = pl.ds(core * RC, RC)
    other = pl.ds((1 - core) * RC, RC)

    def dev(s, ct):
        return {"sample": s, "ctx": ct}

    sibling = dev(s_id + 1 - 2 * core, c)

    def rcopy(src, dst, send, recv, device):
        return pltpu.make_async_remote_copy(
            src_ref=src, dst_ref=dst, send_sem=send, recv_sem=recv,
            device_id=device, device_id_type=pl.DeviceIdType.MESH,
        )

    if Y == 4:
        places = ((0, 0), (0, 1), (1, 0), (3, 0), (1, 1), (2, 0), (2, 1), (3, 1))
    else:
        places = tuple((dy, dz) for dy in range(Y) for dz in range(2))

    def g_dev(p):
        dy, dz = places[p]
        zl2 = zl + dz - 2 * zl * dz
        zh2 = zh + dz - 2 * zh * dz
        return dev(x * 4 + zl2 * 2 + core, ((y + dy) % Y) * 2 + zh2)

    def r_of(j):
        dz = zh + j % 2 - 2 * zh * (j % 2)
        dy = (y + Y - j // 2) % Y
        off = dy * 2 + dz
        place = 0
        for p in range(1, NC):
            at = places[p][0] * 2 + places[p][1]
            differs = ((off + NC - at) % NC + NC - 1) // NC
            place = place + p * (1 - differs)
        return place

    def k_send(p):
        return rcopy(
            kall.at[0, half], kall.at[p, half], ks_s.at[p], ks_r.at[p], g_dev(p)
        )

    def k_hand(p):
        return rcopy(kall.at[p, half], kall.at[p, half], kf_s.at[p], kf_r.at[p], sibling)

    def e_send(buf, ss, rs, p):
        rows = pl.ds((x * 2 + core) * EW, EW)
        return rcopy(buf.at[0, rows], buf.at[p, rows], ss.at[p], rs.at[p], g_dev(p))

    def e_part(buf, lo, xi, ci):
        return buf.at[pl.ds(lo, NC - lo), pl.ds((xi * 2 + ci) * EW, EW)]

    def e_along(buf, lo, ss, rs, t):
        to = dev(((x + t) % X) * 4 + zl * 2 + core, c)
        part = e_part(buf, lo, x, core)
        return rcopy(part, part, ss.at[t], rs.at[t], to)

    def e_hand(buf, lo, ss, rs, t):
        part = e_part(buf, lo, (x + X - t) % X, core)
        return rcopy(part, part, ss.at[t], rs.at[t], sibling)

    def e_share(buf, lo, s1, r1, s2, r2, s3, r3):
        for p in range(lo, NC):
            e_send(buf, s1, r1, p).wait_recv()
        for t in range(1, X):
            e_along(buf, lo, s2, r2, t).start()
        e_hand(buf, lo, s3, r3, 0).start()

    def e_pass_on(buf, lo, s2, r2, s3, r3):
        for t in range(1, X):
            part = e_part(buf, lo, (x + X - t) % X, core)
            rcopy(part, part, s2.at[t], r2.at[t], sibling).wait_recv()
            e_hand(buf, lo, s3, r3, t).start()

    def e_arrive(buf, lo, s3, r3):
        for t in range(X):
            part = e_part(buf, lo, (x + X - t) % X, 1 - core)
            rcopy(part, part, s3.at[t], r3.at[t], sibling).wait_recv()

    def e_end(buf, lo, s1, r1, s2, r2, s3, r3):
        for p in range(lo, NC):
            e_send(buf, s1, r1, p).wait_send()
        for t in range(1, X):
            e_along(buf, lo, s2, r2, t).wait_send()
        for t in range(X):
            e_hand(buf, lo, s3, r3, t).wait_send()

    def own_at(buf, i):
        return buf.at[NC + i // 2, pl.ds((i % 2) * RC, RC)]

    def own_copy(buf, i, send, rs, to_y, to_zh):
        return rcopy(own_at(buf, i), own_at(buf, i), send, rs.at[i], dev(s_id, to_y * 2 + to_zh))

    def own_y(buf, ss, rs):
        return own_copy(buf, c, ss.at[0], rs, (y + 1) % Y, zh)

    def own_wrap(buf, ss, rs):
        return own_copy(buf, c, ss.at[1], rs, Y - 1, zh)

    def own_forward(buf, ss, rs):
        return own_copy(buf, c - 2, ss.at[2], rs, (y + 1) % Y, zh)

    def own_z(buf, zs, rs, yy):
        return own_copy(buf, yy * 2 + zh, zs.at[yy], rs, y, 1 - zh)

    def own_got(buf, rs, i):
        return rcopy(own_at(buf, i), own_at(buf, i), rs.at[i], rs.at[i], sibling)

    def own_start(buf, ss, zs, rs):
        @pl.when(y < Y - 1)
        def _():
            own_y(buf, ss, rs).start()

        if Y > 2:
            @pl.when(y == 0)
            def _():
                own_wrap(buf, ss, rs).start()

        @pl.when(zh == 0)
        def _():
            own_z(buf, zs, rs, y).start()

    def own_next(buf, ss, zs, rs):
        @pl.when(y >= 1)
        def _():
            own_got(buf, rs, c - 2).wait_recv()

            @pl.when(y < Y - 1)
            def _():
                own_forward(buf, ss, rs).start()

            own_z(buf, zs, rs, y - 1).start()

    def own_rest(buf, zs, rs):
        @pl.loop(0, jnp.maximum(y - 1, 0))
        def _(yy):
            own_got(buf, rs, yy * 2 + zh).wait_recv()
            own_z(buf, zs, rs, yy).start()

    def own_end(buf, ss, zs, rs):
        @pl.when(y < Y - 1)
        def _():
            own_y(buf, ss, rs).wait_send()

        if Y > 2:
            @pl.when(y == 0)
            def _():
                own_wrap(buf, ss, rs).wait_send()

        @pl.when((y >= 1) & (y < Y - 1))
        def _():
            own_forward(buf, ss, rs).wait_send()

        @pl.loop(0, y + 1 - zh)
        def _(yy):
            own_z(buf, zs, rs, yy).wait_send()

    barrier = pltpu.get_barrier_semaphore()

    def greet(device):
        pl.semaphore_signal(
            barrier, inc=1, device_id=device, device_id_type=pl.DeviceIdType.MESH
        )

    greet(sibling)
    for t in range(1, NC):
        greet(dev(s_id, (c + t) % NC))
    for p in range(1, NC):
        if places[p][1]:
            greet(g_dev(p))
    for t in range(1, NP):
        greet(dev(((pair + t) % NP) * 2 + core, c))

    kall[0] = pk_ref[...]
    vall[0] = pv_ref[...]
    kall[NC + c // 2, pl.ds((c % 2) * RC, RC)] = rk_ref[0]
    vall[NC + c // 2, pl.ds((c % 2) * RC, RC)] = rv_ref[0]

    @pl.when(c % 2 == 0)
    def _():
        kall[NC + c // 2, RC:] = jnp.zeros((RC, DH), bf16)
        vall[NC + c // 2, RC:] = jnp.zeros((RC, DH), bf16)

    pl.semaphore_wait(barrier, 1 + (NC - 1) + NC // 2 + (NP - 1))

    for p in range(1, NC):
        k_send(p).start()
    own_start(kall, ok_s, oz_s, ok_r)

    ones = jnp.ones((8, DH), bf16)

    def delta(gr, o):
        prod = gr.astype(f32) * o.astype(f32)
        hi = prod.astype(bf16)
        lo = (prod - hi.astype(f32)).astype(bf16)
        return dot(ones, hi, NT) + dot(ones, lo, NT)

    for h in range(H):
        cols = slice(h * DH, (h + 1) * DH)
        rows = slice(h * RC, (h + 1) * RC)
        q[rows] = rq_ref[0, :, cols]
        g[rows] = rg_ref[0, :, cols]
        qp[h * PR : (h + 1) * PR] = pq_ref[:, cols]
        gp[h * PR : (h + 1) * PR] = pg_ref[:, cols]
        D[:, rows] = delta(rg_ref[0, :, cols], ro_ref[0, :, cols])
    prod_o = jnp.concatenate([po_ref[:, h * DH : (h + 1) * DH] for h in range(H)], axis=0)
    Dp[...] = delta(gp[...], prod_o)
    M2[...] = jnp.full_like(M2, MASKED)
    S[...] = jnp.zeros_like(S)
    M2p[...] = jnp.full_like(M2p, MASKED)
    Sp[...] = jnp.zeros_like(Sp)
    dqt[...] = jnp.zeros_like(dqt)
    dqtp[...] = jnp.zeros_like(dqtp)

    def first(i_id, buf, h):
        cols = slice(h * RC, (h + 1) * RC)
        s = dot(kall[i_id], q[cols], NT)
        buf[:, cols] = s
        M2[0, :, cols] = jnp.maximum(
            M2[0, :, cols], jnp.max(s.reshape(KC // 8, 8, RC), axis=0)
        )

    def second(i_id, buf, h):
        cols = slice(h * RC, (h + 1) * RC)
        s = buf[:, cols].reshape(KC // 8, 8, RC)
        new, old = M2[1, :, cols], M2[2, :, cols]
        e = jnp.exp2((s - new) * C)
        S[:, cols] = S[:, cols] * jnp.exp2((old - new) * C) + jnp.sum(e, axis=0)
        E[pl.ds(pl.multiple_of(i_id * KC, KC), KC), cols] = e.reshape(KC, RC).astype(bf16)

    def rotate(i_id):
        M2[2] = M2[1]
        M2[1] = M2[0]
        Mj[i_id] = M2[0]

    values_e = (vall, 1, vs_s, vs_r, vx_s, vx_r, vf_s, vf_r)

    def hand(p):
        mine_ = kall.at[p, half]
        rcopy(mine_, mine_, ks_s.at[p], ks_r.at[p], sibling).wait_recv()
        k_hand(p).start()

    def handed(p):
        part = kall.at[p, other]
        rcopy(part, part, kf_s.at[p], kf_r.at[p], sibling).wait_recv()

    def step(a, b, bufa, bufb):
        for h in range(H):
            first(b, bufb, h)
            second(a, bufa, h)
        rotate(b)

    for h in range(H):
        first(0, SA, h)
    rotate(0)
    hand(1)

    @pl.loop(0, NC // 2 - 1)
    def _(t):
        p = 2 * t

        @pl.when(t == NC // 2 - 2)
        def _():
            own_next(kall, ok_s, oz_s, ok_r)
            for r in range(1, NC):
                e_send(vall, vs_s, vs_r, r).start()

        hand(p + 2)
        handed(p + 1)
        step(p, p + 1, SA, SB)
        hand(p + 3)
        handed(p + 2)
        step(p + 1, p + 2, SB, SA)

    own_rest(kall, oz_s, ok_r)
    handed(NC - 1)
    step(NC - 2, NC - 1, SA, SB)
    for h in range(H):
        second(NC - 1, SB, h)

    def own_weights(i_id, mask):
        for h in range(H):
            cols = slice(h * RC, (h + 1) * RC)
            s = dot(kall[i_id], q[cols], NT)
            if mask is not None:
                s = jnp.where(mask, s, MASKED)
            s = s.reshape(KC // 8, 8, RC)
            old = M2[0, :, cols]
            new = jnp.maximum(old, jnp.max(s, axis=0))
            e = jnp.exp2((s - new) * C)
            S[:, cols] = S[:, cols] * jnp.exp2((old - new) * C) + jnp.sum(e, axis=0)
            E[pl.ds(pl.multiple_of(i_id * KC, KC), KC), cols] = e.reshape(KC, RC).astype(bf16)
            Mj[i_id, :, cols] = new
            M2[0, :, cols] = new

    @pl.when(c % 2 == 1)
    def _():
        own_got(kall, ok_r, c - 1).wait_recv()

    dg = NC + y
    key_at = lax.broadcasted_iota(jnp.int32, (KC, RC), 0)
    row_at = lax.broadcasted_iota(jnp.int32, (KC, RC), 1) + zh * RC
    own_weights(dg, key_at <= row_at)
    e_share(*values_e)
    own_start(vall, ov_s, ow_s, ov_r)

    @pl.loop(0, y)
    def _(jo):
        own_got(kall, ok_r, 2 * jo + 1 - zh).wait_recv()
        own_weights(NC + jo, None)

    @pl.loop(0, jd + 1)
    def _(j):
        s = dot(kall[r_of(j)], qp[...], NT)
        keys = j * KC + lax.broadcasted_iota(jnp.int32, (KC, NPC), 0)
        rows = row0 + lax.broadcasted_iota(jnp.int32, (KC, NPC), 1) % PR
        ok = (keys <= rows).reshape(KC // 8, 8, NPC)
        s = jnp.where(ok, s.reshape(KC // 8, 8, NPC), MASKED)
        old = M2p[...]
        new = jnp.maximum(old, jnp.max(s, axis=0))
        e = jnp.where(ok, jnp.exp2((s - new) * C), 0.0)
        Sp[...] = Sp[...] * jnp.exp2((old - new) * C) + jnp.sum(e, axis=0)
        Ep[pl.ds(pl.multiple_of(j * KC, KC), KC)] = e.reshape(KC, NPC).astype(bf16)
        Mjp[j] = new
        M2p[...] = new

    e_pass_on(vall, 1, vx_s, vx_r, vf_s, vf_r)
    own_next(vall, ov_s, ow_s, ov_r)

    length = len_ref[0]
    live = (c * RC + lax.broadcasted_iota(jnp.int32, (1, NR), 1) % RC) < length
    m = M2[0]
    mt = jnp.max(m, axis=0, keepdims=True)
    st = jnp.sum(S[...] * jnp.exp2((m - mt) * C), axis=0, keepdims=True)
    Mt[...] = mt
    Inv[...] = jnp.where(live, 1.0 / st, 0.0)
    mp = M2p[...]
    mpt = jnp.max(mp, axis=0, keepdims=True)
    invp = 1.0 / jnp.sum(Sp[...] * jnp.exp2((mp - mpt) * C), axis=0, keepdims=True)

    def grads(i_id, between=None):
        base = pl.ds(pl.multiple_of(i_id * KC, KC), KC)
        for h in range(H):
            cols = slice(h * RC, (h + 1) * RC)
            dp = dot(vall[i_id], g[cols], NT)
            w = jnp.exp2((Mj[i_id, :, cols] - Mt[:, cols]) * C) * Inv[:, cols]
            p = (E[base, cols].astype(f32).reshape(KC // 8, 8, RC) * w).astype(bf16)
            p = p.reshape(KC, RC)
            PB[:, cols] = p
            GB[:, cols] = (dp - D[0:1, cols]).astype(bf16) * p
        if between is not None:
            between()
        DKV[1] = dot(PB[...], g[...], NN)
        DKV[0] = dot(GB[...], q[...], NN)
        for h in range(H):
            cols = slice(h * RC, (h + 1) * RC)
            dqt[h] += dot(kall[i_id], GB[:, cols], TN)

    def grads_prompt(j):
        base = pl.ds(pl.multiple_of(j * KC, KC), KC)
        r = r_of(j)
        dp = dot(vall[r], gp[...], NT)
        w = jnp.exp2((Mjp[j] - mpt) * C) * invp
        p = (Ep[base].astype(f32).reshape(KC // 8, 8, NPC) * w).astype(bf16).reshape(KC, NPC)
        ds = (dp - Dp[0:1]).astype(bf16) * p
        DKV[1] += dot(p, gp[...], NN)
        DKV[0] += dot(ds, qp[...], NN)
        dqtp[...] += dot(kall[r], ds, TN)

    e_arrive(vall, 1, vf_s, vf_r)

    def sib_copy(i):
        return rcopy(sibs.at[i], sibr.at[i], sib_s.at[i], sib_r.at[i], sibling)

    def x_send(i):
        to = ((pair + 1 + i) % NP) * 2 + core
        return rcopy(xs.at[i], xr.at[pair], x_s.at[i], x_r.at[pair], dev(to, c))

    mine = pl.ds(zh * RC, RC)
    theirs = pl.ds((1 - zh) * RC, RC)

    def oy_send(jo):
        return rcopy(oy.at[jo], oyr.at[y], oy_s.at[jo], oy_r.at[y], dev(s_id, jo * 2 + zh))

    def oz_send():
        return rcopy(
            os_.at[0], os_.at[1], o_s.at[0], o_r.at[0], dev(s_id, y * 2 + 1 - zh)
        )

    @pl.loop(0, NP)
    def _(i):
        j = (pair + 1 + i) % NP
        def pass_sum():
            @pl.when(i >= 1)
            def _():
                sib_copy(i - 1).wait_recv()
                xs[i - 1] = (keep[i - 1] + sibr[i - 1].astype(f32)).astype(bf16)
                x_send(i - 1).start()

        grads(r_of(j), pass_sum)

        @pl.when(j <= jd)
        def _():
            grads_prompt(j)

        @pl.when(i == 0)
        def _():
            own_rest(vall, ow_s, ov_r)

        keep[i, 0] = DKV[0, half] * scaling
        keep[i, 1] = DKV[1, half]
        sibs[i, 0] = (DKV[0, other] * scaling).astype(bf16)
        sibs[i, 1] = DKV[1, other].astype(bf16)
        sib_copy(i).start()

        @pl.when((i >= 2) & (i < y + 2))
        def _():
            jo = i - 2
            own_got(vall, ov_r, 2 * jo + 1 - zh).wait_recv()
            grads(NC + jo)
            oy[jo, 0] = (DKV[0] * scaling).astype(bf16)
            oy[jo, 1] = DKV[1].astype(bf16)
            oy_send(jo).start()

    def c_send(t):
        to = (c + t) % NC
        return rcopy(cs.at[t], cr.at[c], c_s.at[t], c_r.at[c], dev(s_id, to))

    def sum_prompt():
        sib_copy(NP - 1).wait_recv()
        total = keep[NP - 1] + sibr[NP - 1].astype(f32)
        for t in range(1, NP):
            k = (pair + t) % NP
            rcopy(xr.at[k], xr.at[k], x_s.at[t - 1], x_r.at[k], sibling).wait_recv()
            total = total + xr[k].astype(f32)
        keep[NP - 1] = total

        for t in range(1, NC):
            to = (c + t) % NC
            cs[t] = keep[NP - 1, :, pl.ds(to * PR, PR)].astype(bf16)
            c_send(t).start()

    @pl.when(zh == 1)
    def _():
        own_got(vall, ov_r, c - 1).wait_recv()

    grads(dg, sum_prompt)
    own_keep[0] = DKV[0] * scaling
    own_keep[1] = DKV[1]

    @pl.loop(y + 1, Y)
    def _(yy):
        rcopy(oyr.at[yy], oyr.at[yy], oy_s.at[yy], oy_r.at[yy], sibling).wait_recv()
        own_keep[...] += oyr[yy].astype(f32)

    os_[0] = own_keep[:, theirs].astype(bf16)
    oz_send().start()

    for h in range(H):
        cols = slice(h * DH, (h + 1) * DH)
        drq_ref[0, :, cols] = (dqt[h].T * scaling).astype(bf16)
    dqp = (dqtp[...].T * scaling).astype(bf16)
    for h in range(H):
        dpq_ref[:, h * DH : (h + 1) * DH] = dqp[h * PR : (h + 1) * PR]

    oz_send().wait_recv()
    total = own_keep[:, mine] + os_[1].astype(f32)
    drk_ref[0] = total[0].astype(bf16)
    drv_ref[0] = total[1].astype(bf16)

    total = keep[NP - 1, :, pl.ds(c * PR, PR)]
    for t in range(1, NC):
        k = (c + t) % NC
        rcopy(cr.at[k], cr.at[k], c_s.at[t], c_r.at[k], sibling).wait_recv()
        total = total + cr[k].astype(f32)
    dpk_ref[...] = total[0].astype(bf16)
    dpv_ref[...] = total[1].astype(bf16)

    for r in range(1, NC):
        c_send(r).wait_send()
    for p in range(1, NC):
        k_send(p).wait_send()
        k_hand(p).wait_send()
    e_end(*values_e)
    own_end(kall, ok_s, oz_s, ok_r)
    own_end(vall, ov_s, ow_s, ov_r)
    oz_send().wait_send()

    @pl.loop(0, y)
    def _(jo):
        oy_send(jo).wait_send()

    for i in range(NP):
        sib_copy(i).wait_send()
    for i in range(NP - 1):
        x_send(i).wait_send()


def copy_kernel(*refs):
    for i in range(6):
        refs[6 + i][...] = refs[i][...]


def on_device(NS, NC, *args):
    pq, pk = args[0], args[1]
    rq = args[5]
    DH = pk.shape[1]
    H = pq.shape[1] // DH
    KC, PR, RC = pk.shape[0], pq.shape[0], rq.shape[1]
    NR, NPC, NP, NK = RC * H, PR * H, NS // 2, NC + NC // 2
    vm = pltpu.VMEM
    dma = pltpu.SemaphoreType.DMA
    sds = jax.ShapeDtypeStruct
    scratch = [
        vm((NR, DH), bf16), vm((NR, DH), bf16), vm((NPC, DH), bf16), vm((NPC, DH), bf16),
        vm((NK, KC, DH), bf16), vm((NK, KC, DH), bf16),
        vm((NK * KC, NR), bf16), vm((NC * KC, NPC), bf16),
        vm((KC, NR), f32), vm((KC, NR), f32), vm((KC, NR), bf16), vm((KC, NR), bf16),
        vm((8, 128), bf16), vm((8, 128), bf16),
        vm((3, 8, NR), f32), vm((8, NR), f32), vm((NK, 8, NR), f32), vm((1, NR), f32),
        vm((1, NR), f32), vm((8, NR), f32),
        vm((8, NPC), f32), vm((8, NPC), f32), vm((NC, 8, NPC), f32), vm((8, NPC), f32),
        vm((H, DH, RC), f32), vm((DH, NPC), f32), vm((2, KC, DH), f32),
        vm((NP, 2, RC, DH), f32), vm((NP, 2, RC, DH), bf16), vm((NP, 2, RC, DH), bf16),
        vm((NP, 2, RC, DH), bf16), vm((NP, 2, RC, DH), bf16),
        vm((NC, 2, PR, DH), bf16), vm((NC, 2, PR, DH), bf16),
        vm((2, KC, DH), f32), vm((2, 2, RC, DH), bf16),
        vm((NC // 2, 2, KC, DH), bf16), vm((NC // 2, 2, KC, DH), bf16),
    ]
    scratch += [dma((NC,))] * 16 + [dma((NP,))] * 4 + [dma((NC,))] * 6
    vspec = pl.BlockSpec(memory_space=pltpu.VMEM)
    outs = pl.pallas_call(
        functools.partial(kernel, NS, NC, H, KC, PR),
        out_shape=(
            sds((PR, H * DH), bf16), sds((PR, DH), bf16), sds((PR, DH), bf16),
            sds((1, RC, H * DH), bf16), sds((1, RC, DH), bf16), sds((1, RC, DH), bf16),
        ),
        in_specs=[vspec] * 10 + [pl.BlockSpec(memory_space=pltpu.SMEM)],
        out_specs=[vspec] * 6,
        scratch_shapes=scratch,
        compiler_params=pltpu.CompilerParams(
            collective_id=0, has_side_effects=True, vmem_limit_bytes=62 * 2**20
        ),
    )(*args)
    return pl.pallas_call(
        copy_kernel,
        out_shape=tuple(sds(o.shape, o.dtype) for o in outs),
        in_specs=[vspec] * 6,
        out_specs=[vspec] * 6,
    )(*outs)


def solution(mesh):
    placed = (
        P(("sample", "ctx"), None),
        P("ctx", None),
        P("ctx", None),
        P(("sample", "ctx"), None),
        P(("sample", "ctx"), None),
        P("sample", "ctx", None),
        P("sample", "ctx", None),
        P("sample", "ctx", None),
        P("sample", "ctx", None),
        P("sample", "ctx", None),
        P("sample"),
    )
    return jax.shard_map(
        functools.partial(on_device, mesh.shape["sample"], mesh.shape["ctx"]),
        mesh=mesh,
        in_specs=placed,
        out_specs=(
            P(("sample", "ctx"), None),
            P(("sample", "ctx"), None),
            P(("sample", "ctx"), None),
            P("sample", "ctx", None),
            P("sample", "ctx", None),
            P("sample", "ctx", None),
        ),
        check_vma=False,
    )
```

time: 99.7 us -> 87.5 us (0.88)
  Pallas kernels: 91.9 us -> 85.2 us
  local copies, waits for them, and re-layouts: 6.18 us -> 0 us
    pallas_call x1, Pallas kernels: 91.9 us -> 83.3 us  [on_device(): pl.pallas_call(functools.partial(kernel, NS, NC, H, KC, PR), out_shape=(s...]
    unnamed x14 -> x0, local copies, waits for them, and re-layouts: 6.18 us -> none
    pallas_call x0 -> x1, Pallas kernels: none -> 1.96 us  [on_device(): pl.pallas_call(copy_kernel, out_shape=tuple((sds(o.shape, o.dtype) for o...]
where the time goes in v2:
time: 87.5 us; the launch traced here: 86.5 us
  Pallas kernels  85.2 us (97%)
  between operations  1.29 us (1%)
    pallas_call x1, Pallas kernels, on_device(): pl.pallas_call(functools.partial(kernel, NS, NC, H, KC, PR), out_shape=(s...  83.3 us
    pallas_call x1, Pallas kernels, on_device(): pl.pallas_call(copy_kernel, out_shape=tuple((sds(o.shape, o.dtype) for o...  1.96 us

profile of v2, /device:TPU:6, one launch (start us, length us, event | category | flops | bytes accessed | tf_op | source)
XLA Modules:
  0.0 86.5 jit_solution(11710666926332530075)
XLA Ops:
  1.3 83.3 %shard_map.154 = (bf16[32,1024]{1,0:T(8,128)(2,1)}, bf16[32,128]{1,0:T(8,128)(2,1)}, bf16[32,128]{1,0:T(8,128)(2,1)}, bf16[1,256,1024]{2,1,0:T(8,128)(2,1)}, bf1...) custom-call(bf16[32,1024]{1,0:T(8,128)(2,1)} %pq_ref.1, bf16[512,128]{1,0:T(8,128)(2,1)} %pk_ref.1, ...), custom_call_target="tpu_custom_call" | custom-call | tf_op jit(solution)/shard_map/pallas_call | solution.py:581
  84.5 2.0 %shard_map.155 = (bf16[32,1024]{1,0:T(8,128)(2,1)}, bf16[32,128]{1,0:T(8,128)(2,1)}, bf16[32,128]{1,0:T(8,128)(2,1)}, bf16[1,256,1024]{2,1,0:T(8,128)(2,1)}, bf1...) custom-call(bf16[32,1024]{1,0:T(8,128)(2,1)} %get-tuple-element.12.refs_0_, ...), custom_call_target="tpu_custom_call" | custom-call | tf_op jit(solution)/shard_map/pallas_call | solution.py:594

commit v3 on v2

--- a/solution.py
+++ b/solution.py
@@ -232,9 +232,11 @@
 
     pl.semaphore_wait(barrier, 1 + (NC - 1) + NC // 2 + (NP - 1))
 
-    for p in range(1, NC):
+    for p in range(1, NC // 2):
         k_send(p).start()
     own_start(kall, ok_s, oz_s, ok_r)
+    for p in range(NC // 2, NC):
+        k_send(p).start()
 
     ones = jnp.ones((8, DH), bf16)
 
@@ -353,11 +355,6 @@
     e_share(*values_e)
     own_start(vall, ov_s, ow_s, ov_r)
 
-    @pl.loop(0, y)
-    def _(jo):
-        own_got(kall, ok_r, 2 * jo + 1 - zh).wait_recv()
-        own_weights(NC + jo, None)
-
     @pl.loop(0, jd + 1)
     def _(j):
         s = dot(kall[r_of(j)], qp[...], NT)
@@ -372,6 +369,11 @@
         Ep[pl.ds(pl.multiple_of(j * KC, KC), KC)] = e.reshape(KC, NPC).astype(bf16)
         Mjp[j] = new
         M2p[...] = new
+
+    @pl.loop(0, y)
+    def _(jo):
+        own_got(kall, ok_r, 2 * jo + 1 - zh).wait_recv()
+        own_weights(NC + jo, None)
 
     e_pass_on(vall, 1, vx_s, vx_r, vf_s, vf_r)
     own_next(vall, ov_s, ow_s, ov_r)
@@ -439,14 +441,7 @@
     @pl.loop(0, NP)
     def _(i):
         j = (pair + 1 + i) % NP
-        def pass_sum():
-            @pl.when(i >= 1)
-            def _():
-                sib_copy(i - 1).wait_recv()
-                xs[i - 1] = (keep[i - 1] + sibr[i - 1].astype(f32)).astype(bf16)
-                x_send(i - 1).start()
-
-        grads(r_of(j), pass_sum)
+        grads(r_of(j))
 
         @pl.when(j <= jd)
         def _():
@@ -461,6 +456,12 @@
         sibs[i, 0] = (DKV[0, other] * scaling).astype(bf16)
         sibs[i, 1] = DKV[1, other].astype(bf16)
         sib_copy(i).start()
+
+        @pl.when(i >= 1)
+        def _():
+            sib_copy(i - 1).wait_recv()
+            xs[i - 1] = (keep[i - 1] + sibr[i - 1].astype(f32)).astype(bf16)
+            x_send(i - 1).start()
 
         @pl.when((i >= 2) & (i < y + 2))
         def _():

time: 87.5 us -> 85.8 us (0.981)
  Pallas kernels: 85.2 us -> 83.8 us
    pallas_call x1, Pallas kernels: 83.3 us -> 81.9 us  [on_device(): pl.pallas_call(functools.partial(kernel, NS, NC, H, KC, PR), out_shape=(s...]
where the time goes in v3:
time: 85.8 us; the launch traced here: 85.1 us
  Pallas kernels  83.8 us (98%)
  between operations  1.29 us (2%)
    pallas_call x1, Pallas kernels, on_device(): pl.pallas_call(functools.partial(kernel, NS, NC, H, KC, PR), out_shape=(s...  81.9 us
    pallas_call x1, Pallas kernels, on_device(): pl.pallas_call(copy_kernel, out_shape=tuple((sds(o.shape, o.dtype) for o...  1.96 us

profile of v3, /device:TPU:6, one launch (start us, length us, event | category | flops | bytes accessed | tf_op | source)
XLA Modules:
  0.0 85.1 jit_solution(14115811206202833241)
XLA Ops:
  1.3 81.9 %shard_map.154 = (bf16[32,1024]{1,0:T(8,128)(2,1)}, bf16[32,128]{1,0:T(8,128)(2,1)}, bf16[32,128]{1,0:T(8,128)(2,1)}, bf16[1,256,1024]{2,1,0:T(8,128)(2,1)}, bf1...) custom-call(bf16[32,1024]{1,0:T(8,128)(2,1)} %pq_ref.1, bf16[512,128]{1,0:T(8,128)(2,1)} %pk_ref.1, ...), custom_call_target="tpu_custom_call" | custom-call | tf_op jit(solution)/shard_map/pallas_call | solution.py:582
  83.2 2.0 %shard_map.155 = (bf16[32,1024]{1,0:T(8,128)(2,1)}, bf16[32,128]{1,0:T(8,128)(2,1)}, bf16[32,128]{1,0:T(8,128)(2,1)}, bf16[1,256,1024]{2,1,0:T(8,128)(2,1)}, bf1...) custom-call(bf16[32,1024]{1,0:T(8,128)(2,1)} %get-tuple-element.12.refs_0_, ...), custom_call_target="tpu_custom_call" | custom-call | tf_op jit(solution)/shard_map/pallas_call | solution.py:595

commit v4 on v3

--- a/solution.py
+++ b/solution.py
@@ -232,10 +232,8 @@
 
     pl.semaphore_wait(barrier, 1 + (NC - 1) + NC // 2 + (NP - 1))
 
-    for p in range(1, NC // 2):
-        k_send(p).start()
     own_start(kall, ok_s, oz_s, ok_r)
-    for p in range(NC // 2, NC):
+    for p in range(1, NC):
         k_send(p).start()
 
     ones = jnp.ones((8, DH), bf16)
@@ -301,34 +299,6 @@
             second(a, bufa, h)
         rotate(b)
 
-    for h in range(H):
-        first(0, SA, h)
-    rotate(0)
-    hand(1)
-
-    @pl.loop(0, NC // 2 - 1)
-    def _(t):
-        p = 2 * t
-
-        @pl.when(t == NC // 2 - 2)
-        def _():
-            own_next(kall, ok_s, oz_s, ok_r)
-            for r in range(1, NC):
-                e_send(vall, vs_s, vs_r, r).start()
-
-        hand(p + 2)
-        handed(p + 1)
-        step(p, p + 1, SA, SB)
-        hand(p + 3)
-        handed(p + 2)
-        step(p + 1, p + 2, SB, SA)
-
-    own_rest(kall, oz_s, ok_r)
-    handed(NC - 1)
-    step(NC - 2, NC - 1, SA, SB)
-    for h in range(H):
-        second(NC - 1, SB, h)
-
     def own_weights(i_id, mask):
         for h in range(H):
             cols = slice(h * RC, (h + 1) * RC)
@@ -339,6 +309,8 @@
             old = M2[0, :, cols]
             new = jnp.maximum(old, jnp.max(s, axis=0))
             e = jnp.exp2((s - new) * C)
+            if mask is not None:
+                e = jnp.where(mask.reshape(KC // 8, 8, RC), e, 0.0)
             S[:, cols] = S[:, cols] * jnp.exp2((old - new) * C) + jnp.sum(e, axis=0)
             E[pl.ds(pl.multiple_of(i_id * KC, KC), KC), cols] = e.reshape(KC, RC).astype(bf16)
             Mj[i_id, :, cols] = new
@@ -352,6 +324,35 @@
     key_at = lax.broadcasted_iota(jnp.int32, (KC, RC), 0)
     row_at = lax.broadcasted_iota(jnp.int32, (KC, RC), 1) + zh * RC
     own_weights(dg, key_at <= row_at)
+    M2[1] = M2[0]
+    for h in range(H):
+        first(0, SA, h)
+    rotate(0)
+    hand(1)
+
+    @pl.loop(0, NC // 2 - 1)
+    def _(t):
+        p = 2 * t
+
+        @pl.when(t == NC // 2 - 2)
+        def _():
+            own_next(kall, ok_s, oz_s, ok_r)
+            for r in range(1, NC):
+                e_send(vall, vs_s, vs_r, r).start()
+
+        hand(p + 2)
+        handed(p + 1)
+        step(p, p + 1, SA, SB)
+        hand(p + 3)
+        handed(p + 2)
+        step(p + 1, p + 2, SB, SA)
+
+    own_rest(kall, oz_s, ok_r)
+    handed(NC - 1)
+    step(NC - 2, NC - 1, SA, SB)
+    for h in range(H):
+        second(NC - 1, SB, h)
+
     e_share(*values_e)
     own_start(vall, ov_s, ow_s, ov_r)
 

time: 85.8 us -> 85.4 us (level)
  no operation moved by 1% of the time
where the time goes in v4:
time: 85.4 us; the launch traced here: 84.8 us
  Pallas kernels  83.5 us (98%)
  between operations  1.29 us (2%)
    pallas_call x1, Pallas kernels, on_device(): pl.pallas_call(functools.partial(kernel, NS, NC, H, KC, PR), out_shape=(s...  81.5 us
    pallas_call x1, Pallas kernels, on_device(): pl.pallas_call(copy_kernel, out_shape=tuple((sds(o.shape, o.dtype) for o...  1.96 us

profile of v4, /device:TPU:6, one launch (start us, length us, event | category | flops | bytes accessed | tf_op | source)
XLA Modules:
  0.0 84.8 jit_solution(10005146042568010410)
XLA Ops:
  1.3 81.5 %shard_map.154 = (bf16[32,1024]{1,0:T(8,128)(2,1)}, bf16[32,128]{1,0:T(8,128)(2,1)}, bf16[32,128]{1,0:T(8,128)(2,1)}, bf16[1,256,1024]{2,1,0:T(8,128)(2,1)}, bf1...) custom-call(bf16[32,1024]{1,0:T(8,128)(2,1)} %pq_ref.1, bf16[512,128]{1,0:T(8,128)(2,1)} %pk_ref.1, ...), custom_call_target="tpu_custom_call" | custom-call | tf_op jit(solution)/shard_map/pallas_call | solution.py:583
  82.8 2.0 %shard_map.155 = (bf16[32,1024]{1,0:T(8,128)(2,1)}, bf16[32,128]{1,0:T(8,128)(2,1)}, bf16[32,128]{1,0:T(8,128)(2,1)}, bf16[1,256,1024]{2,1,0:T(8,128)(2,1)}, bf1...) custom-call(bf16[32,1024]{1,0:T(8,128)(2,1)} %get-tuple-element.12.refs_0_, ...), custom_call_target="tpu_custom_call" | custom-call | tf_op jit(solution)/shard_map/pallas_call | solution.py:596
